TPU v7x, 512 devices: a whole 4x8x8 slice. The times are simulated.
512 devices in a mesh: row: 32 (over z, x_hi, core), col: 16 (over x_lo, y).
Axes of the slice: x: 4 (x_hi: 2, x_lo: 2; x = x_hi * 2 + x_lo), y: 8, z: 8, core: 2. Of those that a mesh axis runs over, the one named last changes fastest.
Arguments:
- trunk_in: bfloat16 [1536, 32768], P('col', 'row'), may hold values from -24 to 24
- conv_weight: bfloat16 [5, 1536, 1536], P(None, 'col'), may hold values from -0.0625 to 0.0625
- conv_bias: float32 [1536], P('col'), may hold values from -3 to 3
- norm_gain: float32 [1536], replicated, may hold values from 0.1 to 1.9
- pair_proj: bfloat16 [64, 1536], replicated, may hold values from -0.15625 to 0.15625
- pair_in: bfloat16 [2048, 512, 128], P('row', 'col'), may hold values from -6 to 6
- opm_weight: bfloat16 [1024, 128], replicated, may hold values from -0.1875 to 0.1875
- pair_bias: float32 [128], replicated, may hold values from -3 to 3
Outputs:
- trunk_out: bfloat16 [1536, 32768], P('col', 'row')
- pair_out: bfloat16 [2048, 512, 128], P('row', 'col')
All inputs are finite; a program needn't handle non-finite values.
Results may differ from a plain program's by a relative error of at most 0.012.
Values may be sent and summed in bfloat16 or wider, within the bound.
A program may use at most 64 MiB of HBM per device.

v0:
```python
import jax
import jax.numpy as jnp
from jax import lax
from jax.sharding import PartitionSpec as P

TRUNK_CHANNELS = 1536
DILATION_STEP = 8
POOL = 16
OPM = 32
WINDOWS = 4
EPSILON = 1e-05


def with_halo(cells, sides, width):
    for axis, dim in sides:
        count = lax.axis_size(axis)
        ends = count - 1
        head = lax.slice_in_dim(cells, 0, width, axis=dim)
        tail = lax.slice_in_dim(cells, cells.shape[dim] - width, cells.shape[dim], axis=dim)
        cells = jnp.concatenate(
            [
                lax.ppermute(tail, axis, [(i, (i + 1) % count) for i in range(ends)]),
                cells,
                lax.ppermute(head, axis, [((i + 1) % count, i) for i in range(ends)]),
            ],
            axis=dim,
        )
    return cells


def partner_2(block, axis, bit):
    count = lax.axis_size(axis)
    route = []
    for low in range(count):
        high = low | 1 << bit
        if high != low and high < count:
            route += [(low, high), (high, low)]
    return lax.ppermute(block, axis, route)


def per_device(
    trunk_in, conv_weight, conv_bias, norm_gain, pair_proj, pair_in, opm_weight, pair_bias
):
    local_channels = trunk_in.shape[0]
    token_positions = trunk_in.shape[1]
    kernel = conv_weight.shape[0]
    border_width = 2 * DILATION_STEP
    per_window = lax.axis_size("row") // WINDOWS
    row_index = lax.axis_index("row")
    col_index = lax.axis_index("col")
    in_window = row_index % per_window
    source = trunk_in.astype(jnp.float32)
    zero_sum = jnp.zeros((local_channels, token_positions), jnp.float32)
    gathered = lax.all_gather(trunk_in, "col", axis=0, tiled=True)
    padded_trunk = with_halo(gathered, (("row", 1),), border_width)
    values = padded_trunk.astype(jnp.float32)
    scale = lax.rsqrt(jnp.mean(values * values, axis=0, keepdims=True) + EPSILON)
    gelu_output = jax.nn.gelu(values * norm_gain[:, None] * scale).astype(jnp.bfloat16)
    conv_sum = zero_sum
    for tap_offset in range(kernel):
        conv_sum = conv_sum + jnp.dot(
            conv_weight[tap_offset],
            gelu_output[
                :, tap_offset * DILATION_STEP : tap_offset * DILATION_STEP + token_positions
            ],
            preferred_element_type=jnp.float32,
        )
    trunk_out = (source + conv_sum + conv_bias[:, None]).astype(jnp.bfloat16)
    pooled = (
        trunk_out.astype(jnp.float32)
        .reshape(local_channels, token_positions // POOL, POOL)
        .mean(axis=2)
        .astype(jnp.bfloat16)
    )
    own_proj = lax.dynamic_slice_in_dim(pair_proj, col_index * local_channels, local_channels, 1)
    pooled_f = pooled.astype(jnp.float32)
    partial_proj = lax.dot_general(
        pooled, own_proj, (((0,), (1,)), ((), ())), preferred_element_type=jnp.float32
    )
    projected, sums = lax.psum((partial_proj, jnp.sum(pooled_f * pooled_f, axis=0)), "col")
    sides = (projected * lax.rsqrt(sums / TRUNK_CHANNELS + EPSILON)[:, None]).astype(jnp.bfloat16)
    row_side = sides[:, :OPM]
    collected = sides[:, OPM:]
    col_block = pair_in.shape[1]
    pooled_rows = row_side.shape[0]
    for bit_num in range(per_window.bit_length() - 1):
        partner = partner_2(collected, "row", bit_num)
        upper_half = in_window // 2**bit_num % 2 == 1
        collected = jnp.where(
            upper_half,
            jnp.concatenate([partner, collected], axis=0),
            jnp.concatenate([collected, partner], axis=0),
        )
    own_cols = lax.dynamic_slice_in_dim(collected, col_index * col_block, col_block, 0)
    outer = (
        row_side.astype(jnp.float32)[:, None, :, None]
        * own_cols.astype(jnp.float32)[None, :, None, :]
    ).astype(jnp.bfloat16)
    outer = outer.reshape(pooled_rows * col_block, OPM * OPM)
    update = jnp.dot(outer, opm_weight, preferred_element_type=jnp.float32).reshape(pair_in.shape)
    pair_out = (pair_in.astype(jnp.float32) + update + pair_bias).astype(jnp.bfloat16)
    return (trunk_out, pair_out)


def solution(mesh):
    return jax.shard_map(
        per_device,
        mesh=mesh,
        in_specs=(
            P("col", "row"),
            P(None, "col", None),
            P("col"),
            P(),
            P(),
            P("row", "col", None),
            P(),
            P(),
        ),
        out_specs=(P("col", "row"), P("row", "col", None)),
        check_vma=False,
    )
```

profile of v0, /device:TPU:64, one launch (start us, length us, event | category | flops | bytes accessed | tf_op | source)
XLA Modules:
  0.0 214.4 jit_solution(7731478625536114508)
XLA Ops:
  7.2 0.7 all-gather.2.cloned.1.call-update
  7.9 83.4 %all-gather.2.cloned.1.call-done = bf16[1536,1024]{1,0:T(8,128)(2,1)} async-done(((bf16[96,1024]{1,0:T(8,128)(2,1)}), bf16[1536,1024]{1,0:T(8,128)(2,1)}) %all-gather.2.cloned.1.call-update) | async-done | bytes 3145744 | tf_op jit(solution)/shard_map/all_gather | solution.py:54
  91.3 1.3 fusion.69
  92.6 1.9 collective-permute-start
  94.5 6.0 %collective-permute-start.1 = (bf16[1536,16]{1,0:T(8,128)(2,1)S(1)}, bf16[1536,16]{1,0:T(8,128)(2,1)S(1)}, u32[]{:S(2)}, u32[]{:S(2)}) collective-permute-start(bf16[1536,16]{1,0:T(8,128)(2,1)S(1)} %get-tuple-element.4), channel_id=1, source_target_pairs={{16,0},{32,16},{48,32},{64,48},{80,64},{96,80},{112,96},{128,112},... | collective-permute-start | bytes 147464 | tf_op jit(solution)/shard_map/ppermute | solution.py:24
  100.6 3.5 %collective-permute-done = bf16[1536,16]{1,0:T(8,128)(2,1)S(1)} collective-permute-done((bf16[1536,16]{1,0:T(8,128)(2,1)S(1)}, bf16[1536,16]{1,0:T(8,128)(2,1)S(1)}, u32[]{:S(2)}, u32[]{:S(2)}) %collective-permute-start) | collective-permute-done | bytes 49184 | tf_op jit(solution)/shard_map/ppermute | solution.py:22
  104.1 1.7 collective-permute-done.1
  105.9 7.5 %concatenate.21 = bf16[1536,1056]{1,0:T(8,128)(2,1)} concatenate(bf16[1536,16]{1,0:T(8,128)(2,1)S(1)} %collective-permute-done, bf16[1536,1024]{1,0:T(8,128)(2,1)} %all-gather.2.cloned.1.call-done, bf16[1536,16]{1,0:T(8,128)(2,1)S(1)} %collective-permute-done.1), dimensions={1} | concatenate | bytes 6488064 | tf_op jit(solution)/shard_map/concatenate | solution.py:20
  113.4 2.9 %fusion.8 = f32[1056]{0:T(1024)S(1)} fusion(bf16[1536,1056]{1,0:T(8,128)(2,1)} %concatenate.21), kind=kLoop, calls=%fused_computation.12 | loop fusion | flops 4864992 | bytes 3248256 | tf_op jit(solution)/shard_map/reduce_sum | solution.py:57
  116.3 0.1 copy-done.1
  116.4 3.7 %fusion.3 = bf16[1536,1056]{1,0:T(8,128)(2,1)S(1)} fusion(bf16[1536,1056]{1,0:T(8,128)(2,1)S(1)} %copy-done.1, f32[1056]{0:T(1024)S(1)} %add_rsqrt_fusion, f32[1536]{0:T(1024)S(1)} %copy-done.5), kind=kLoop, calls=%fused_computation.7 | loop fusion | flops 19464192 | bytes 6498432 | tf_op jit(solution)/shard_map/convert_element_type | solution.py:58
  120.1 1.1 fusion.13
  121.3 1.1 fusion.15
  122.4 1.1 fusion.17
  123.6 1.1 fusion.19
  124.8 0.7 fusion.47
  125.5 0.1 copy.21
  125.6 0.1 bitcast_reduce_fusion
  125.7 0.1 multiply_reduce_fusion
  125.8 1.0 fusion.61
  126.8 62.4 %all-reduce = (f32[64,64]{0,1:T(8,128)S(1)}, f32[64]{0:T(128)S(1)}) all-reduce(f32[64,64]{0,1:T(8,128)S(1)} %fusion.61, f32[64]{0:T(128)S(1)} %multiply_reduce_fusion), channel_id=1, replica_groups=mesh['row'=32,'col'=16] {'col'}, use_global_device_ids=true, to_apply=%region_2.3 | all-reduce | flops 4160 | bytes 33280 | tf_op jit(solution)/shard_map/psum | solution.py:80
  189.2 1.9 collective-permute-start.2
  191.2 1.1 collective-permute-done.2
  192.3 0.1 maximum_select_fusion.1
  192.3 4.5 %collective-permute-start.3 = (bf16[128,32]{0,1:T(8,128)(2,1)S(1)}, bf16[128,32]{0,1:T(8,128)(2,1)S(1)}, u32[]{:S(2)}, u32[]{:S(2)}) collective-permute-start(bf16[128,32]{0,1:T(8,128)(2,1)S(1)} %maximum_select_fusion.1), channel_id=1, source_target_pairs={{0,32},{32,0},{16,48},{48,16},{64,96},{96,64},{80,112},{112,80},{1... | collective-permute-start | bytes 24584 | tf_op jit(solution)/shard_map/ppermute | solution.py:38
  196.9 2.5 %collective-permute-done.3 = bf16[128,32]{0,1:T(8,128)(2,1)S(1)} collective-permute-done((bf16[128,32]{0,1:T(8,128)(2,1)S(1)}, bf16[128,32]{0,1:T(8,128)(2,1)S(1)}, u32[]{:S(2)}, u32[]{:S(2)}) %collective-permute-start.3) | collective-permute-done | bytes 8224 | tf_op jit(solution)/shard_map/ppermute | solution.py:38
  199.4 1.9 collective-permute-start.4
  201.4 0.2 copy.23
  201.6 3.4 %collective-permute-done.4 = bf16[256,32]{0,1:T(8,128)(2,1)S(1)} collective-permute-done((bf16[256,32]{0,1:T(8,128)(2,1)S(1)}, bf16[256,32]{0,1:T(8,128)(2,1)S(1)}, u32[]{:S(2)}, u32[]{:S(2)}) %collective-permute-start.4) | collective-permute-done | bytes 16416 | tf_op jit(solution)/shard_map/ppermute | solution.py:38
  205.0 0.1 fusion.65
  205.2 0.2 mul.101
  205.5 2.1 fusion.25
  (26 shorter events, 0.3 us)
Async XLA Ops:
  7.2 198.3 %copy-start = (bf16[1024,128]{1,0:T(8,128)(2,1)S(1)}, bf16[1024,128]{1,0:T(8,128)(2,1)}, u32[]{:S(2)}) copy-start(bf16[1024,128]{1,0:T(8,128)(2,1)} %param.14) | copy-start | bytes 786436
  7.2 84.1 %all-gather.2.cloned.1.call-start = ((), (), s32[]{:S(2)}) async-start(), calls=%async_computation | async-start | bytes 3342336 | tf_op jit(solution)/shard_map/all_gather | solution.py:54
  92.6 11.5 %collective-permute-start = (bf16[1536,16]{1,0:T(8,128)(2,1)S(1)}, bf16[1536,16]{1,0:T(8,128)(2,1)S(1)}, u32[]{:S(2)}, u32[]{:S(2)}) collective-permute-start(bf16[1536,16]{1,0:T(8,128)(2,1)S(1)} %get-tuple-element.5), channel_id=1, source_target_pairs={{0,16},{16,32},{32,48},{48,64},{64,80},{80,96},{96,112},{112,128},... | collective-permute-start | bytes 147464 | tf_op jit(solution)/shard_map/ppermute | solution.py:22
  94.5 11.3 %collective-permute-start.1 = (bf16[1536,16]{1,0:T(8,128)(2,1)S(1)}, bf16[1536,16]{1,0:T(8,128)(2,1)S(1)}, u32[]{:S(2)}, u32[]{:S(2)}) collective-permute-start(bf16[1536,16]{1,0:T(8,128)(2,1)S(1)} %get-tuple-element.4), channel_id=1, source_target_pairs={{16,0},{32,16},{48,32},{64,48},{80,64},{96,80},{112,96},{128,112},... | collective-permute-start | bytes 147464 | tf_op jit(solution)/shard_map/ppermute | solution.py:24
  113.3 3.1 %copy-start.1 = (bf16[1536,1056]{1,0:T(8,128)(2,1)S(1)}, bf16[1536,1056]{1,0:T(8,128)(2,1)}, u32[]{:S(2)}) copy-start(bf16[1536,1056]{1,0:T(8,128)(2,1)} %concatenate.21) | copy-start | bytes 9732100
  113.3 3.1 %copy-start.5 = (f32[1536]{0:T(1024)S(1)}, f32[1536]{0:T(1024)}, u32[]{:S(2)}) copy-start(f32[1536]{0:T(1024)} %param.11) | copy-start | bytes 18436
  116.4 3.7 %copy-start.4 = (bf16[5,96,1536]{2,1,0:T(8,128)(2,1)S(1)}, bf16[5,96,1536]{2,1,0:T(8,128)(2,1)}, u32[]{:S(2)}) copy-start(bf16[5,96,1536]{2,1,0:T(8,128)(2,1)} %param.9) | copy-start | bytes 4423684
  122.4 2.3 %copy-start.2 = (bf16[96,1024]{1,0:T(8,128)(2,1)S(1)}, bf16[96,1024]{1,0:T(8,128)(2,1)}, u32[]{:S(2)}) copy-start(bf16[96,1024]{1,0:T(8,128)(2,1)} %param.8) | copy-start | bytes 589828
  122.4 2.3 %copy-start.6 = (f32[96]{0:T(128)S(1)}, f32[96]{0:T(128)}, u32[]{:S(2)}) copy-start(f32[96]{0:T(128)} %param.10) | copy-start | bytes 1156
  124.7 80.7 %copy-start.7 = (bf16[64,32,128]{2,1,0:T(8,128)(2,1)S(1)}, bf16[64,32,128]{2,1,0:T(8,128)(2,1)}, u32[]{:S(2)}) copy-start(bf16[64,32,128]{2,1,0:T(8,128)(2,1)} %param.13) | copy-start | bytes 1572868
  124.7 80.7 %copy-start.8 = (f32[128]{0:T(128)S(1)}, f32[128]{0:T(128)}, u32[]{:S(2)}) copy-start(f32[128]{0:T(128)} %param.15) | copy-start | bytes 1540
  125.5 82.1 %copy-start.3 = (bf16[96,1024]{1,0:T(8,128)(2,1)}, bf16[96,1024]{1,0:T(8,128)(2,1)S(1)}, u32[]{:S(2)}) copy-start(bf16[96,1024]{1,0:T(8,128)(2,1)S(1)} %fusion.47) | copy-start | bytes 589828
  189.2 3.1 %collective-permute-start.2 = (bf16[64,32]{0,1:T(8,128)(2,1)S(1)}, bf16[64,32]{0,1:T(8,128)(2,1)S(1)}, u32[]{:S(2)}, u32[]{:S(2)}) collective-permute-start(bf16[64,32]{0,1:T(8,128)(2,1)S(1)} %get-tuple-element.7), channel_id=1, source_target_pairs={{0,16},{16,0},{32,48},{48,32},{64,80},{80,64},{96,112},{112,96},{1... | collective-permute-start | bytes 12296 | tf_op jit(solution)/shard_map/ppermute | solution.py:38
  192.3 7.0 %collective-permute-start.3 = (bf16[128,32]{0,1:T(8,128)(2,1)S(1)}, bf16[128,32]{0,1:T(8,128)(2,1)S(1)}, u32[]{:S(2)}, u32[]{:S(2)}) collective-permute-start(bf16[128,32]{0,1:T(8,128)(2,1)S(1)} %maximum_select_fusion.1), channel_id=1, source_target_pairs={{0,32},{32,0},{16,48},{48,16},{64,96},{96,64},{80,112},{112,80},{1... | collective-permute-start | bytes 24584 | tf_op jit(solution)/shard_map/ppermute | solution.py:38
  199.4 5.6 %collective-permute-start.4 = (bf16[256,32]{0,1:T(8,128)(2,1)S(1)}, bf16[256,32]{0,1:T(8,128)(2,1)S(1)}, u32[]{:S(2)}, u32[]{:S(2)}) collective-permute-start(bf16[256,32]{0,1:T(8,128)(2,1)S(1)} %maximum_select_fusion), channel_id=1, source_target_pairs={{0,64},{64,0},{16,80},{80,16},{32,96},{96,32},{48,112},{112,48},{1... | collective-permute-start | bytes 49160 | tf_op jit(solution)/shard_map/ppermute | solution.py:38
Sparse Core Ops, SparseCore 0:
  10.1 81.1 all-gather.1
where the time goes:
time: 215 us; the launch traced here: 214 us
  waiting for transfers between devices  96.4 us (45%)
  blocking collectives  62.4 us (29%)
  starting transfers between devices  16.3 us (8%)
  between operations  14.4 us (7%)
  local copies, waits for them, and re-layouts  9.64 us (4%)
  matrix products  8.25 us (4%)
  other arithmetic  7.03 us (3%)
    all_gather x1, waiting for transfers between devices, per_device(): gathered = lax.all_gather(trunk_in, 'col', axis=0, tiled=True)  83.4 us
    psum x1, blocking collectives, per_device(): lax.psum((partial_proj, jnp.sum(pooled_f * pooled_f, axis=0)), 'col')  62.4 us
    ppermute x3, starting transfers between devices, partner_2(): return lax.ppermute(block, axis, route)  8.33 us
    concatenate x1, local copies, waits for them, and re-layouts, with_halo(): jnp.concatenate([lax.ppermute(tail, axis, [(i, (i + 1) % count) for i in...  7.49 us
    ppermute x3, waiting for transfers between devices, partner_2(): return lax.ppermute(block, axis, route)  7.02 us
    ppermute x1, starting transfers between devices, with_halo(): lax.ppermute(head, axis, [((i + 1) % count, i) for i in range(ends)])  6.05 us
    dot_general x5, matrix products, per_device(): jnp.dot(conv_weight[tap_offset], gelu_output[:, tap_offset * DILATION_STE...  5.25 us
  transfers between devices with their start and end apart: 6, of which 6 were waited for; matrix products, arithmetic and copies ran while one was open for 0% of the time, Pallas kernels for 0%

commit v1 on v0

--- a/solution.py
+++ b/solution.py
@@ -51,7 +51,9 @@
     in_window = row_index % per_window
     source = trunk_in.astype(jnp.float32)
     zero_sum = jnp.zeros((local_channels, token_positions), jnp.float32)
-    gathered = lax.all_gather(trunk_in, "col", axis=0, tiled=True)
+    gathered = jnp.concatenate(
+        lax.all_to_all(jnp.stack([trunk_in] * lax.axis_size("col")), "col", 0, 0), axis=0
+    )
     padded_trunk = with_halo(gathered, (("row", 1),), border_width)
     values = padded_trunk.astype(jnp.float32)
     scale = lax.rsqrt(jnp.mean(values * values, axis=0, keepdims=True) + EPSILON)

time: 215 us -> 200 us (0.930)
  the two profiles are of different devices: /device:TPU:64 before, /device:TPU:256 now
where the time goes in v1:
time: 200 us; the launch traced here: 199 us
  blocking collectives  142 us (71%)
  starting transfers between devices  17.7 us (9%)
  waiting for transfers between devices  12.4 us (6%)
  local copies, waits for them, and re-layouts  10 us (5%)
  matrix products  8.27 us (4%)
  other arithmetic  7.01 us (4%)
    all_to_all x1, blocking collectives, per_device(): lax.all_to_all(jnp.stack([trunk_in] * lax.axis_size('col')), 'col', 0, 0)  79.8 us
    psum x1, blocking collectives, per_device(): lax.psum((partial_proj, jnp.sum(pooled_f * pooled_f, axis=0)), 'col')  62.5 us
    ppermute x3, starting transfers between devices, partner_2(): return lax.ppermute(block, axis, route)  8.55 us
    ppermute x1, starting transfers between devices, with_halo(): lax.ppermute(head, axis, [((i + 1) % count, i) for i in range(ends)])  7.26 us
    ppermute x3, waiting for transfers between devices, partner_2(): return lax.ppermute(block, axis, route)  6.8 us
    concatenate x1, local copies, waits for them, and re-layouts, with_halo(): jnp.concatenate([lax.ppermute(tail, axis, [(i, (i + 1) % count) for i in...  6.72 us
    dot_general x5, matrix products, per_device(): jnp.dot(conv_weight[tap_offset], gelu_output[:, tap_offset * DILATION_STE...  5.26 us
  transfers between devices with their start and end apart: 5, of which 5 were waited for; matrix products, arithmetic and copies ran while one was open for 0% of the time, Pallas kernels for 0%

profile of v1, /device:TPU:256, one launch (start us, length us, event | category | flops | bytes accessed | tf_op | source)
XLA Modules:
  0.0 198.7 jit_solution(9955061636600635783)
XLA Ops:
  0.6 1.4 stack.2
  2.0 79.8 %all_to_all.5 = bf16[16,96,1024]{2,1,0:T(8,128)(2,1)S(1)} all-to-all(bf16[16,96,1024]{2,1,0:T(8,128)(2,1)S(1)} %stack.2), channel_id=1, replica_groups=mesh['row'=32,'col'=16] {'col'}, dimensions={0} | all-to-all | bytes 6291456 | tf_op jit(solution)/shard_map/all_to_all | solution.py:55
  81.8 1.1 fusion.69
  82.9 1.9 collective-permute-start
  84.8 7.3 %collective-permute-start.1 = (bf16[1536,16]{1,0:T(8,128)(2,1)}, bf16[1536,16]{1,0:T(8,128)(2,1)}, u32[]{:S(2)}, u32[]{:S(2)}) collective-permute-start(bf16[1536,16]{1,0:T(8,128)(2,1)} %get-tuple-element.4), channel_id=1, source_target_pairs={{16,0},{32,16},{48,32},{64,48},{80,64},{96,80},{112,96},{128,112},... | collective-permute-start | bytes 147464 | tf_op jit(solution)/shard_map/ppermute | solution.py:24
  92.1 3.9 %collective-permute-done = bf16[1536,16]{1,0:T(8,128)(2,1)} collective-permute-done((bf16[1536,16]{1,0:T(8,128)(2,1)}, bf16[1536,16]{1,0:T(8,128)(2,1)}, u32[]{:S(2)}, u32[]{:S(2)}) %collective-permute-start) | collective-permute-done | bytes 49184 | tf_op jit(solution)/shard_map/ppermute | solution.py:22
  96.0 1.7 collective-permute-done.1
  97.7 6.7 %concatenate.21 = bf16[1536,1056]{1,0:T(8,128)(2,1)} concatenate(bf16[1536,16]{1,0:T(8,128)(2,1)} %collective-permute-done, bf16[1536,1024]{1,0:T(8,128)(2,1)S(1)} %bitcast.31, bf16[1536,16]{1,0:T(8,128)(2,1)} %collective-permute-done.1), dimensions={1} | concatenate | bytes 6488064 | tf_op jit(solution)/shard_map/concatenate | solution.py:20
  104.4 2.9 %fusion.8 = f32[1056]{0:T(1024)S(1)} fusion(bf16[1536,1056]{1,0:T(8,128)(2,1)} %concatenate.21), kind=kLoop, calls=%fused_computation.12 | loop fusion | flops 4864992 | bytes 3248256 | tf_op jit(solution)/shard_map/reduce_sum | solution.py:59
  107.3 0.1 copy-done.1
  107.5 3.7 %fusion.3 = bf16[1536,1056]{1,0:T(8,128)(2,1)S(1)} fusion(bf16[1536,1056]{1,0:T(8,128)(2,1)S(1)} %copy-done.1, f32[1056]{0:T(1024)S(1)} %add_rsqrt_fusion, f32[1536]{0:T(1024)S(1)} %copy-done.5), kind=kLoop, calls=%fused_computation.7 | loop fusion | flops 19464192 | bytes 6498432 | tf_op jit(solution)/shard_map/convert_element_type | solution.py:60
  111.1 1.1 fusion.13
  112.3 1.1 fusion.15
  113.5 1.1 fusion.17
  114.6 1.1 fusion.19
  115.8 0.7 fusion.47
  116.5 0.1 copy.40
  116.7 0.1 bitcast_reduce_fusion
  116.8 0.1 multiply_reduce_fusion
  116.9 1.0 fusion.61
  117.8 62.5 %all-reduce = (f32[64,64]{0,1:T(8,128)S(1)}, f32[64]{0:T(128)S(1)}) all-reduce(f32[64,64]{0,1:T(8,128)S(1)} %fusion.61, f32[64]{0:T(128)S(1)} %multiply_reduce_fusion), channel_id=1, replica_groups=mesh['row'=32,'col'=16] {'col'}, use_global_device_ids=true, to_apply=%region_2.3 | all-reduce | flops 4160 | bytes 33280 | tf_op jit(solution)/shard_map/psum | solution.py:82
  180.4 1.9 collective-permute-start.2
  182.3 1.1 collective-permute-done.2
  183.4 0.1 maximum_select_fusion.1
  183.5 4.5 %collective-permute-start.3 = (bf16[128,32]{0,1:T(8,128)(2,1)S(1)}, bf16[128,32]{0,1:T(8,128)(2,1)S(1)}, u32[]{:S(2)}, u32[]{:S(2)}) collective-permute-start(bf16[128,32]{0,1:T(8,128)(2,1)S(1)} %maximum_select_fusion.1), channel_id=1, source_target_pairs={{0,32},{32,0},{16,48},{48,16},{64,96},{96,64},{80,112},{112,80},{1... | collective-permute-start | bytes 24584 | tf_op jit(solution)/shard_map/ppermute | solution.py:38
  188.0 2.5 %collective-permute-done.3 = bf16[128,32]{0,1:T(8,128)(2,1)S(1)} collective-permute-done((bf16[128,32]{0,1:T(8,128)(2,1)S(1)}, bf16[128,32]{0,1:T(8,128)(2,1)S(1)}, u32[]{:S(2)}, u32[]{:S(2)}) %collective-permute-start.3) | collective-permute-done | bytes 8224 | tf_op jit(solution)/shard_map/ppermute | solution.py:38
  190.6 2.2 %collective-permute-start.4 = (bf16[256,32]{0,1:T(8,128)(2,1)S(1)}, bf16[256,32]{0,1:T(8,128)(2,1)S(1)}, u32[]{:S(2)}, u32[]{:S(2)}) collective-permute-start(bf16[256,32]{0,1:T(8,128)(2,1)S(1)} %maximum_select_fusion), channel_id=1, source_target_pairs={{0,64},{64,0},{16,80},{80,16},{32,96},{96,32},{48,112},{112,48},{1... | collective-permute-start | bytes 49160 | tf_op jit(solution)/shard_map/ppermute | solution.py:38
  192.8 0.2 copy.42
  193.0 3.2 %collective-permute-done.4 = bf16[256,32]{0,1:T(8,128)(2,1)S(1)} collective-permute-done((bf16[256,32]{0,1:T(8,128)(2,1)S(1)}, bf16[256,32]{0,1:T(8,128)(2,1)S(1)}, u32[]{:S(2)}, u32[]{:S(2)}) %collective-permute-start.4) | collective-permute-done | bytes 16416 | tf_op jit(solution)/shard_map/ppermute | solution.py:38
  196.2 0.1 fusion.65
  196.4 0.2 mul.101
  196.7 2.1 %fusion.25 = bf16[64,32,128]{2,1,0:T(8,128)(2,1)} fusion(f32[32,1024]{1,0:T(8,128)S(1)} %mul.101, f32[64,1024]{1,0:T(8,128)S(1)} %copy.42, bf16[64,32,128]{2,1,0:T(8,128)(2,1)S(1)} %copy-done.7, f32[128]{0:T(128)S(1)} %copy-done.8, bf16[1024,128]{1,0:T(8,128)(2,1)S(1)} %copy-done), kind=kOutput, calls=%fused_computation.29 | convolution fusion | flops 542113792 | bytes 1704448 | tf_op jit(solution)/shard_map/dot_general | solution.py:102
  (25 shorter events, 0.2 us)
Async XLA Ops:
  0.6 196.0 %copy-start = (bf16[1024,128]{1,0:T(8,128)(2,1)S(1)}, bf16[1024,128]{1,0:T(8,128)(2,1)}, u32[]{:S(2)}) copy-start(bf16[1024,128]{1,0:T(8,128)(2,1)} %param.14) | copy-start | bytes 786436
  82.9 13.1 %collective-permute-start = (bf16[1536,16]{1,0:T(8,128)(2,1)}, bf16[1536,16]{1,0:T(8,128)(2,1)}, u32[]{:S(2)}, u32[]{:S(2)}) collective-permute-start(bf16[1536,16]{1,0:T(8,128)(2,1)} %get-tuple-element.5), channel_id=1, source_target_pairs={{0,16},{16,32},{32,48},{48,64},{64,80},{80,96},{96,112},{112,128},... | collective-permute-start | bytes 147464 | tf_op jit(solution)/shard_map/ppermute | solution.py:22
  84.8 12.9 %collective-permute-start.1 = (bf16[1536,16]{1,0:T(8,128)(2,1)}, bf16[1536,16]{1,0:T(8,128)(2,1)}, u32[]{:S(2)}, u32[]{:S(2)}) collective-permute-start(bf16[1536,16]{1,0:T(8,128)(2,1)} %get-tuple-element.4), channel_id=1, source_target_pairs={{16,0},{32,16},{48,32},{64,48},{80,64},{96,80},{112,96},{128,112},... | collective-permute-start | bytes 147464 | tf_op jit(solution)/shard_map/ppermute | solution.py:24
  104.4 3.1 %copy-start.1 = (bf16[1536,1056]{1,0:T(8,128)(2,1)S(1)}, bf16[1536,1056]{1,0:T(8,128)(2,1)}, u32[]{:S(2)}) copy-start(bf16[1536,1056]{1,0:T(8,128)(2,1)} %concatenate.21) | copy-start | bytes 9732100
  104.4 3.1 %copy-start.5 = (f32[1536]{0:T(1024)S(1)}, f32[1536]{0:T(1024)}, u32[]{:S(2)}) copy-start(f32[1536]{0:T(1024)} %param.11) | copy-start | bytes 18436
  107.4 3.7 %copy-start.4 = (bf16[5,96,1536]{2,1,0:T(8,128)(2,1)S(1)}, bf16[5,96,1536]{2,1,0:T(8,128)(2,1)}, u32[]{:S(2)}) copy-start(bf16[5,96,1536]{2,1,0:T(8,128)(2,1)} %param.9) | copy-start | bytes 4423684
  113.4 2.3 %copy-start.2 = (bf16[96,1024]{1,0:T(8,128)(2,1)S(1)}, bf16[96,1024]{1,0:T(8,128)(2,1)}, u32[]{:S(2)}) copy-start(bf16[96,1024]{1,0:T(8,128)(2,1)} %param.8) | copy-start | bytes 589828
  113.4 2.3 %copy-start.6 = (f32[96]{0:T(128)S(1)}, f32[96]{0:T(128)}, u32[]{:S(2)}) copy-start(f32[96]{0:T(128)} %param.10) | copy-start | bytes 1156
  115.8 80.9 %copy-start.7 = (bf16[64,32,128]{2,1,0:T(8,128)(2,1)S(1)}, bf16[64,32,128]{2,1,0:T(8,128)(2,1)}, u32[]{:S(2)}) copy-start(bf16[64,32,128]{2,1,0:T(8,128)(2,1)} %param.13) | copy-start | bytes 1572868
  115.8 80.9 %copy-start.8 = (f32[128]{0:T(128)S(1)}, f32[128]{0:T(128)}, u32[]{:S(2)}) copy-start(f32[128]{0:T(128)} %param.15) | copy-start | bytes 1540
  116.5 82.2 %copy-start.3 = (bf16[96,1024]{1,0:T(8,128)(2,1)}, bf16[96,1024]{1,0:T(8,128)(2,1)S(1)}, u32[]{:S(2)}) copy-start(bf16[96,1024]{1,0:T(8,128)(2,1)S(1)} %fusion.47) | copy-start | bytes 589828
  180.4 3.1 %collective-permute-start.2 = (bf16[64,32]{0,1:T(8,128)(2,1)S(1)}, bf16[64,32]{0,1:T(8,128)(2,1)S(1)}, u32[]{:S(2)}, u32[]{:S(2)}) collective-permute-start(bf16[64,32]{0,1:T(8,128)(2,1)S(1)} %get-tuple-element.7), channel_id=1, source_target_pairs={{0,16},{16,0},{32,48},{48,32},{64,80},{80,64},{96,112},{112,96},{1... | collective-permute-start | bytes 12296 | tf_op jit(solution)/shard_map/ppermute | solution.py:38
  183.5 7.0 %collective-permute-start.3 = (bf16[128,32]{0,1:T(8,128)(2,1)S(1)}, bf16[128,32]{0,1:T(8,128)(2,1)S(1)}, u32[]{:S(2)}, u32[]{:S(2)}) collective-permute-start(bf16[128,32]{0,1:T(8,128)(2,1)S(1)} %maximum_select_fusion.1), channel_id=1, source_target_pairs={{0,32},{32,0},{16,48},{48,16},{64,96},{96,64},{80,112},{112,80},{1... | collective-permute-start | bytes 24584 | tf_op jit(solution)/shard_map/ppermute | solution.py:38
  190.6 5.6 %collective-permute-start.4 = (bf16[256,32]{0,1:T(8,128)(2,1)S(1)}, bf16[256,32]{0,1:T(8,128)(2,1)S(1)}, u32[]{:S(2)}, u32[]{:S(2)}) collective-permute-start(bf16[256,32]{0,1:T(8,128)(2,1)S(1)} %maximum_select_fusion), channel_id=1, source_target_pairs={{0,64},{64,0},{16,80},{80,16},{32,96},{96,32},{48,112},{112,48},{1... | collective-permute-start | bytes 49160 | tf_op jit(solution)/shard_map/ppermute | solution.py:38
